TPU v7x, 512 devices: a whole 4x8x8 slice. The times are simulated.
512 devices in a mesh: expert: 64 (over x, y, core), store: 8 (over z).
Axes of the slice: x: 4, y: 8, z: 8, core: 2. Of those that a mesh axis runs over, the one named last changes fastest.
Arguments:
- tokens: bfloat16 [65536, 2048], P(('expert', 'store')), may hold values from -6 to 6
- chosen_expert_index: int32 [65536, 8], P(('expert', 'store')), may hold values from 0 to 63, all different within a row; in each aligned block of 128 rows (0 to 127, 128 to 255, ...) at most 18 rows name the same one
- router_weight_logits: float32 [65536, 8], P(('expert', 'store')), may hold values from 0.1 to 1
- token_tenant_index: int32 [65536], P(('expert', 'store')), may hold values from 0 to 7
- adapted: int32 [8, 64], P(None, 'expert'), may hold values 0 or 1
- gate_up_weight: bfloat16 [64, 2048, 768], P('expert', 'store'), may hold values from -0.125 to 0.125
- down_weight: bfloat16 [64, 384, 2048], P('expert', None, 'store'), may hold values from -0.3125 to 0.3125
- adapter_input_factors: bfloat16 [8, 64, 32, 2048], P('store', 'expert'), may hold values from -0.125 to 0.125
- adapter_output_factors: bfloat16 [8, 64, 32, 384], P('store', 'expert'), may hold values from -0.8984375 to 0.8984375
Outputs:
- mixed: bfloat16 [65536, 2048], P(('expert', 'store'))
Inputs may be any that keep to these rules, and one draw needn't show every extreme that they name: `chosen_expert_index`: each row names 8 different experts; within the rows of one device no expert is named by more than 18 rows.
All inputs are finite; a program needn't handle non-finite values. No bound on the sum of `adapted` on one device may be relied on, other than what follows from the above.
Results may differ from a plain program's by a relative error of at most 0.006.
Values may be sent and summed in bfloat16 or wider, within the bound.
A program may use at most 128 MiB of HBM per device.

v0:
```python
import jax
import jax.numpy as jnp
from jax import lax
from jax.sharding import PartitionSpec as P


def in_one_piece(arrays, axis, dim, along):
    widths = [a.shape[along] for a in arrays]
    both = jnp.concatenate(arrays, axis=along)
    result = lax.all_gather(both, axis, axis=dim, tiled=True)
    return tuple(jnp.split(result, [sum(widths[:k]) for k in range(1, len(widths))], axis=along))


def widen_factors(factor_up):
    rank_half = factor_up.shape[1] // 2
    hidden = factor_up.shape[2]
    zeros_part = jnp.zeros((factor_up.shape[0], rank_half, hidden), factor_up.dtype)
    upper = jnp.concatenate([factor_up[:, :rank_half], zeros_part], axis=2)
    lower = jnp.concatenate([zeros_part, factor_up[:, rank_half:]], axis=2)
    return jnp.concatenate([upper, lower], axis=1).reshape(-1, 2 * hidden)


def adapter_term(flat_rows, tenant_codes, factor_in, factor_up, adapted_col):
    tenants = factor_in.shape[0]
    rank_full = factor_in.shape[1]
    model_width = factor_in.shape[2]
    low_rank = lax.dot_general(
        flat_rows,
        factor_in.reshape(-1, model_width),
        (((1,), (1,)), ((), ())),
        preferred_element_type=jnp.float32,
    )
    chooser = (
        (tenant_codes[:, None] == jnp.arange(tenants, dtype=jnp.int32)[None, :])
        * adapted_col[None, :]
    ).astype(jnp.float32)
    low_rank = (
        (low_rank.reshape(-1, tenants, rank_full) * chooser[:, :, None])
        .reshape(flat_rows.shape[0], -1)
        .astype(jnp.bfloat16)
    )
    return jnp.dot(low_rank, widen_factors(factor_up), preferred_element_type=jnp.float32)


def adapter_pick(flat_rows, tenant_codes, factor_in, factor_up, adapted_col):
    return adapter_term(flat_rows, tenant_codes, factor_in, factor_up, adapted_col)


def gated(pre_act, hidden):
    return (jax.nn.silu(pre_act[:, :hidden]) * pre_act[:, hidden:]).astype(jnp.bfloat16)


def shards(
    tokens,
    chosen_expert_index,
    router_weight_logits,
    token_tenant_index,
    adapted,
    gate_up_weight,
    down_weight,
    adapter_input_factors,
    adapter_output_factors,
):
    tok_count, model_width = tokens.shape
    top_count = chosen_expert_index.shape[1]
    owners = lax.axis_size("expert")
    slot_cap = max(2, tok_count * top_count * 9 // (8 * owners))
    hidden = down_weight.shape[1]
    flat_ids = chosen_expert_index.reshape(-1)
    onehot = (flat_ids[:, None] == jnp.arange(owners, dtype=jnp.int32)[None, :]).astype(jnp.int32)
    position = jnp.sum((jnp.cumsum(onehot, axis=0) - 1) * onehot, axis=1)
    slot_of = flat_ids * slot_cap + position
    route_token = jnp.arange(tok_count * top_count, dtype=jnp.int32) // top_count
    slot_token = jnp.full((owners * slot_cap,), tok_count, jnp.int32).at[slot_of].set(route_token)
    padded = jnp.concatenate([tokens, jnp.zeros((1, model_width), tokens.dtype)])
    send_rows = padded[slot_token].reshape(owners, slot_cap, model_width)
    tenant_pad = jnp.concatenate([token_tenant_index, jnp.full((1,), -1, jnp.int32)])
    send_codes = tenant_pad[slot_token].astype(jnp.bfloat16).reshape(owners, slot_cap)
    adapted_col = adapted[:, 0]
    weight_in, weight_out, factor_in, factor_up = (
        lax.all_gather(gate_up_weight, "store", axis=1, tiled=True),
        lax.all_gather(down_weight, "store", axis=2, tiled=True),
        *in_one_piece((adapter_input_factors, adapter_output_factors), "store", 0, 3),
    )
    row_block = lax.all_to_all(send_rows, "expert", split_axis=0, concat_axis=0, tiled=True)
    code_block = lax.all_to_all(send_codes, "expert", split_axis=0, concat_axis=0, tiled=True)
    sources = row_block.shape[0]
    slot_count = row_block.shape[1]
    flat_rows = row_block.reshape(-1, model_width)
    tenant_codes = code_block.reshape(-1).astype(jnp.int32)
    pre_act = jnp.dot(flat_rows, weight_in[0], preferred_element_type=jnp.float32)
    pre_act = pre_act + adapter_pick(
        flat_rows, tenant_codes, factor_in[:, 0], factor_up[:, 0], adapted_col
    )
    activation = gated(pre_act, hidden)
    expert_out = jnp.dot(activation, weight_out[0], preferred_element_type=jnp.float32).astype(
        jnp.bfloat16
    )
    returned = lax.all_to_all(
        expert_out.reshape(sources, slot_count, model_width),
        "expert",
        split_axis=0,
        concat_axis=0,
        tiled=True,
    )
    picked = returned.reshape(-1, model_width)[slot_of].reshape(tok_count, top_count, model_width)
    shares = router_weight_logits / jnp.sum(router_weight_logits, axis=1, keepdims=True)
    mixed = jnp.sum(picked.astype(jnp.float32) * shares[:, :, None], axis=1)
    return mixed.astype(jnp.bfloat16)


def solution(mesh):
    placed = (
        P(("expert", "store"), None),
        P(("expert", "store"), None),
        P(("expert", "store"), None),
        P(("expert", "store")),
        P(None, "expert"),
        P("expert", "store", None),
        P("expert", None, "store"),
        P("store", "expert", None, None),
        P("store", "expert", None, None),
    )
    return jax.shard_map(
        shards, mesh=mesh, in_specs=placed, out_specs=P(("expert", "store"), None), check_vma=False
    )
```

profile of v0, /device:TPU:1, one launch (start us, length us, event | category | flops | bytes accessed | tf_op | source)
XLA Modules:
  0.0 444.1 jit_solution(16142490670896120633)
XLA Ops:
  6.5 0.8 copy.22
  7.3 0.1 eq.46
  7.4 0.1 eq.42
  7.5 0.7 broadcast_multiply_fusion
  8.2 18.0 %reduce-window.6 = s32[64,8,128]{2,1,0:T(8,128)S(1)} reduce-window(s32[64,8,128]{2,1,0:T(8,128)S(1)} %fusion.18, s32[]{:T(128)} %constant.36.clone.1), window={size=1x1x128 pad=0_0x0_0x127_0}, to_apply=%region_0.0 | reduce-window | flops 8323072 | bytes 524292 | tf_op jit(solution)/shard_map/reduce-window
  26.2 0.1 slice.30
  26.4 0.1 copy.24
  26.6 0.1 copy.25
  26.6 0.1 add_add_fusion
  26.8 0.1 copy.21
  26.9 0.1 mul.54
  27.0 0.1 fusion.17
  27.1 4.3 scatter_custom_fusion
  31.4 0.7 pad_add_fusion
  32.1 0.0 copy-start
  32.1 7.2 %gather_fusion.1 = s32[1152]{0:T(1024)S(1)} fusion(s32[129]{0:T(256)S(1)} %pad_add_fusion, s32[2048]{0:T(1024)S(1)} %pad_clamp_fusion), kind=kCustom, calls=%fused_computation.1 | custom fusion | bytes 13824 | tf_op jit(solution)/shard_map/gather | solution.py:78
  39.4 0.8 convert_element_type.70
  40.1 11.6 %all-to-all-start.1 = ((bf16[64,1,18]{2,1,0:T(2,128)(2,1)}), bf16[64,1,18]{2,1,0:T(2,128)(2,1)S(1)}, u32[]{:S(2)}, u32[]{:S(2)}) async-start(bf16[64,1,18]{2,1,0:T(2,128)(2,1)} %convert_element_type.70), calls=%async_computation.1 | async-start | bytes 65536 | tf_op jit(solution)/shard_map/all_to_all | solution.py:86
  51.8 0.0 copy-done
  51.8 5.9 %gather_fusion = bf16[1152,2048]{1,0:T(8,128)(2,1)} fusion(bf16[129,2048]{1,0:T(8,128)(2,1)S(1)} %concatenate.18, s32[2048]{0:T(1024)S(1)} %pad_clamp_fusion), kind=kCustom, calls=%fused_computation | custom fusion | bytes 9441792 | tf_op jit(solution)/shard_map/gather | solution.py:76
  57.8 7.5 %reshape.131 = bf16[64,18,2048]{2,1,0:T(8,128)(2,1)} reshape(bf16[1152,2048]{1,0:T(8,128)(2,1)} %gather_fusion) | data formatting | bytes 9437184 | tf_op jit(solution)/shard_map/reshape | solution.py:76
  65.3 0.0 copy-start.1
  65.3 0.0 copy-start.3
  65.3 0.0 copy-start.5
  65.3 0.0 all-to-all-done.1
  65.3 10.6 %all-to-all-start = ((bf16[64,18,2048]{2,1,0:T(8,128)(2,1)}), bf16[64,18,2048]{2,1,0:T(8,128)(2,1)}, u32[]{:S(2)}, u32[]{:S(2)}) async-start(bf16[64,18,2048]{2,1,0:T(8,128)(2,1)} %reshape.131), calls=%async_computation | async-start | bytes 12582912 | tf_op jit(solution)/shard_map/all_to_all | solution.py:85
  76.0 0.0 all-gather.6.cloned.1.call-start
  76.0 0.0 copy-done.1
  76.0 0.0 copy-done.3
  76.0 0.7 pad_maximum_fusion
  76.7 0.0 all-gather.6.cloned.1.call-update
  76.7 0.0 all-gather.4.cloned.1.call-start
  76.8 0.7 all-gather.4.cloned.1.call-update
  77.5 0.2 all-gather.8.cloned.1.call-start
  77.7 0.5 all-gather.8.cloned.1.call-update
  78.2 0.1 convert_reduce_fusion
  78.3 0.1 reshape.135
  78.5 0.0 copy-done.5
  78.5 0.1 select_convert_fusion
  78.5 43.4 %all-gather.6.cloned.1.call-done = bf16[8,1,32,2432]{3,2,1,0:T(8,128)(2,1)} async-done(((bf16[1,1,32,2432]{3,2,1,0:T(8,128)(2,1)}), bf16[8,1,32,2432]{3,2,1,0:T(8,128)(2,1)}) %all-gather.6.cloned.1.call-update) | async-done | bytes 1245200 | tf_op jit(solution)/shard_map/all_gather | solution.py:10
  121.9 0.9 slice_bitcast_fusion.3
  122.9 93.9 %all-to-all-done = bf16[64,18,2048]{2,1,0:T(8,128)(2,1)} async-done(((bf16[64,18,2048]{2,1,0:T(8,128)(2,1)}), bf16[64,18,2048]{2,1,0:T(8,128)(2,1)}, u32[]{:S(2)}, u32[]{:S(2)}) %all-to-all-start) | async-done | bytes 4718624 | tf_op jit(solution)/shard_map/all_to_all | solution.py:85
  216.8 7.7 %reshape.171 = bf16[1152,2048,1]{1,0,2:T(8,128)(2,1)} reshape(bf16[64,18,2048]{2,1,0:T(8,128)(2,1)} %all-to-all-done) | data formatting | bytes 9437184 | tf_op jit(solution)/shard_map/reshape | solution.py:89
  224.5 0.0 copy-start.2
  224.5 7.9 %reshape.132 = bf16[1152,2048]{1,0:T(8,128)(2,1)} reshape(bf16[64,18,2048]{2,1,0:T(8,128)(2,1)} %all-to-all-done) | data formatting | bytes 9437184 | tf_op jit(solution)/shard_map/reshape | solution.py:89
  232.4 0.0 copy-done.2
  232.4 6.6 %convolution_bitcast_fusion = f32[1152,768]{1,0:T(8,128)} fusion(bf16[1152,2048,1]{1,0,2:T(8,128)(2,1)} %reshape.171, bf16[8,1,32,2432]{3,2,0,1:T(8,128)(2,1)S(1)} %bitcast.40, f32[1152,8]{0,1:T(8,128)S(1)} %select_convert_fusion, bf16[8,16,384]{2,1,0:T(8,128)(2,1)S(1)} %get-tuple-element.6, bf16[8,16,384]{2,1,0:T(8,128)(2,1)S(1)} %get-tuple-element.5), kind=kOutput, calls=%fused_computation.8 | convolution fusion | flops 1663107072 | bytes 9539584 | tf_op jit(solution)/shard_map/dot_general | solution.py:42
  239.0 0.0 all-gather.4.cloned.1.call-done
  239.0 9.9 %convolution_add_fusion = f32[1152,768]{1,0:T(8,128)} fusion(f32[1152,768]{1,0:T(8,128)} %convolution_bitcast_fusion, bf16[1152,2048]{1,0:T(8,128)(2,1)} %reshape.132, bf16[1,2048,768]{2,1,0:T(8,128)(2,1)} %all-gather.4.cloned.1.call-done), kind=kOutput, calls=%fused_computation.7 | convolution fusion | flops 3624763392 | bytes 14942208 | tf_op jit(solution)/shard_map/dot_general | solution.py:91
  248.9 0.0 all-gather.8.cloned.1.call-done
  248.9 7.3 %convolution_convert_fusion = bf16[1152,2048]{1,0:T(8,128)(2,1)} fusion(bf16[1,384,2048]{2,1,0:T(8,128)(2,1)} %all-gather.8.cloned.1.call-done, f32[1152,768]{1,0:T(8,128)} %convolution_add_fusion), kind=kOutput, calls=%fused_computation.6 | convolution fusion | flops 1816952832 | bytes 9830400 | tf_op jit(solution)/shard_map/dot_general | solution.py:96
  256.2 7.6 %reshape.133 = bf16[64,18,2048]{2,1,0:T(8,128)(2,1)} reshape(bf16[1152,2048]{1,0:T(8,128)(2,1)} %convolution_convert_fusion) | data formatting | bytes 9437184 | tf_op jit(solution)/shard_map/reshape | solution.py:100
  263.8 0.0 copy-start.4
  263.8 6.1 %all-to-all-start.2 = ((bf16[64,18,2048]{2,1,0:T(8,128)(2,1)}), bf16[64,18,2048]{2,1,0:T(8,128)(2,1)}, u32[]{:S(2)}, u32[]{:S(2)}) async-start(bf16[64,18,2048]{2,1,0:T(8,128)(2,1)} %reshape.133), calls=%async_computation.2 | async-start | bytes 12582912 | tf_op jit(solution)/shard_map/all_to_all | solution.py:99
  269.9 0.0 copy-done.4
  269.9 0.1 copy.29
  270.1 140.7 %all-to-all-done.2 = bf16[64,18,2048]{2,1,0:T(8,128)(2,1)} async-done(((bf16[64,18,2048]{2,1,0:T(8,128)(2,1)}), bf16[64,18,2048]{2,1,0:T(8,128)(2,1)}, u32[]{:S(2)}, u32[]{:S(2)}) %all-to-all-start.2) | async-done | bytes 4718624 | tf_op jit(solution)/shard_map/all_to_all | solution.py:99
  410.7 7.8 %reshape.134 = bf16[1152,2048]{1,0:T(8,128)(2,1)} reshape(bf16[64,18,2048]{2,1,0:T(8,128)(2,1)} %all-to-all-done.2) | data formatting | bytes 9437184 | tf_op jit(solution)/shard_map/reshape | solution.py:106
  418.5 11.8 %gather_fusion.2 = bf16[1024,2048]{1,0:T(8,128)(2,1)} fusion(bf16[1152,2048]{1,0:T(8,128)(2,1)} %reshape.134, s32[1024]{0:T(1024)S(1)} %broadcast_clamp_fusion), kind=kCustom, calls=%fused_computation.2 | custom fusion | bytes 8392704 | tf_op jit(solution)/shard_map/gather | solution.py:106
  430.3 7.3 %fusion = bf16[128,2048]{1,0:T(8,128)(2,1)} fusion(bf16[1024,2048]{1,0:T(8,128)(2,1)} %gather_fusion.2, f32[128,8]{1,0:T(8,128)S(1)} %copy.29), kind=kLoop, calls=%fused_computation.5 | loop fusion | flops 6029312 | bytes 4722688 | tf_op jit(solution)/shard_map/reduce_sum | solution.py:108
  (13 shorter events, 0.2 us)
Async XLA Ops:
  32.1 19.7 %copy-start = (bf16[128,2048]{1,0:T(8,128)(2,1)S(1)}, bf16[128,2048]{1,0:T(8,128)(2,1)}, u32[]{:S(2)}) copy-start(bf16[128,2048]{1,0:T(8,128)(2,1)} %param.9) | copy-start | bytes 1572868
  40.1 25.2 %all-to-all-start.1 = ((bf16[64,1,18]{2,1,0:T(2,128)(2,1)}), bf16[64,1,18]{2,1,0:T(2,128)(2,1)S(1)}, u32[]{:S(2)}, u32[]{:S(2)}) async-start(bf16[64,1,18]{2,1,0:T(2,128)(2,1)} %convert_element_type.70), calls=%async_computation.1 | async-start | bytes 65536 | tf_op jit(solution)/shard_map/all_to_all | solution.py:86
  65.3 10.7 %copy-start.1 = (bf16[1,1,32,2048]{3,2,1,0:T(8,128)(2,1)S(1)}, bf16[1,1,32,2048]{3,2,1,0:T(8,128)(2,1)}, u32[]{:S(2)}) copy-start(bf16[1,1,32,2048]{3,2,1,0:T(8,128)(2,1)} %param.16) | copy-start | bytes 393220
  65.3 10.7 %copy-start.3 = (bf16[1,1,32,384]{3,2,1,0:T(8,128)(2,1)S(1)}, bf16[1,1,32,384]{3,2,1,0:T(8,128)(2,1)}, u32[]{:S(2)}) copy-start(bf16[1,1,32,384]{3,2,1,0:T(8,128)(2,1)} %param.17) | copy-start | bytes 73732
  65.3 13.2 %copy-start.5 = (s32[8,1]{0,1:T(1,128)S(1)}, s32[8,1]{0,1:T(1,128)}, u32[]{:S(2)}) copy-start(s32[8,1]{0,1:T(1,128)} %param.13) | copy-start | bytes 100
  65.3 151.5 %all-to-all-start = ((bf16[64,18,2048]{2,1,0:T(8,128)(2,1)}), bf16[64,18,2048]{2,1,0:T(8,128)(2,1)}, u32[]{:S(2)}, u32[]{:S(2)}) async-start(bf16[64,18,2048]{2,1,0:T(8,128)(2,1)} %reshape.131), calls=%async_computation | async-start | bytes 12582912 | tf_op jit(solution)/shard_map/all_to_all | solution.py:85
  76.0 46.0 %all-gather.6.cloned.1.call-start = ((), (), s32[]{:S(2)}) async-start(), calls=%async_computation.4 | async-start | bytes 1400832 | tf_op jit(solution)/shard_map/all_gather | solution.py:10
  76.7 162.3 %all-gather.4.cloned.1.call-start = ((), (), s32[]{:S(2)}) async-start(), calls=%async_computation.3 | async-start | bytes 3538944 | tf_op jit(solution)/shard_map/all_gather | solution.py:81
  77.5 171.4 %all-gather.8.cloned.1.call-start = ((), (), s32[]{:S(2)}) async-start(), calls=%async_computation.5 | async-start | bytes 1769472 | tf_op jit(solution)/shard_map/all_gather | solution.py:82
  224.5 7.9 %copy-start.2 = (bf16[8,1,32,2432]{3,2,1,0:T(8,128)(2,1)S(1)}, bf16[8,1,32,2432]{3,2,1,0:T(8,128)(2,1)}, u32[]{:S(2)}) copy-start(bf16[8,1,32,2432]{3,2,1,0:T(8,128)(2,1)} %all-gather.6.cloned.1.call-done) | copy-start | bytes 3735556
  263.8 6.1 %copy-start.4 = (f32[128,8]{0,1:T(8,128)S(1)}, f32[128,8]{0,1:T(8,128)}, u32[]{:S(2)}) copy-start(f32[128,8]{0,1:T(8,128)} %param.11) | copy-start | bytes 12292
  263.8 147.0 %all-to-all-start.2 = ((bf16[64,18,2048]{2,1,0:T(8,128)(2,1)}), bf16[64,18,2048]{2,1,0:T(8,128)(2,1)}, u32[]{:S(2)}, u32[]{:S(2)}) async-start(bf16[64,18,2048]{2,1,0:T(8,128)(2,1)} %reshape.133), calls=%async_computation.2 | async-start | bytes 12582912 | tf_op jit(solution)/shard_map/all_to_all | solution.py:99
Sparse Core Ops, SparseCore 0:
  78.9 43.0 all-gather.5
  124.0 50.0 all-gather.3
  176.1 41.2 all-gather.7
where the time goes:
time: 445 us; the launch traced here: 444 us
  waiting for transfers between devices  279 us (63%)
  local copies, waits for them, and re-layouts  71.3 us (16%)
  starting transfers between devices  28.7 us (6%)
  other arithmetic  27.9 us (6%)
  matrix products  23.8 us (5%)
  between operations  13.3 us (3%)
    all_to_all x1, waiting for transfers between devices, shards(): lax.all_to_all(expert_out.reshape(sources, slot_count, model_width), 'exp...  141 us
    all_to_all x1, waiting for transfers between devices, shards(): lax.all_to_all(send_rows, 'expert', split_axis=0, concat_axis=0, tiled=True)  93.9 us
    all_gather x1, waiting for transfers between devices, in_one_piece(): result = lax.all_gather(both, axis, axis=dim, tiled=True)  43.4 us
    another operation x2, other arithmetic  18 us
    reshape x2, local copies, waits for them, and re-layouts, shards(): flat_rows = row_block.reshape(-1, model_width)  15.6 us
    gather x1, local copies, waits for them, and re-layouts, shards(): returned.reshape(-1, model_width)[slot_of]  11.8 us
    all_to_all x1, starting transfers between devices, shards(): lax.all_to_all(send_codes, 'expert', split_axis=0, concat_axis=0, tiled=T...  11.6 us
    all_to_all x1, starting transfers between devices, shards(): lax.all_to_all(send_rows, 'expert', split_axis=0, concat_axis=0, tiled=True)  10.6 us
  transfers between devices with their start and end apart: 6, of which 3 were waited for; matrix products, arithmetic and copies ran while one was open for 11% of the time, Pallas kernels for 0%

commit v1 on v0

v1 whole, which is shorter than its diff:
```python
import functools

import jax
import jax.numpy as jnp
from jax import lax
from jax.experimental import pallas as pl
from jax.experimental.pallas import tpu as pltpu
from jax.sharding import PartitionSpec as P

MESH = pl.DeviceIdType.MESH
NX, NY, NC = 4, 8, 2
PEERS = NX * NC
SLOTS = 18
TILE = 16
CHUNKS = 8
GROUP = 4
F32, BF16 = jnp.float32, jnp.bfloat16


def dot(a, b, dims=((1,), (0,))):
    return lax.dot_general(a, b, (dims, ((), ())), preferred_element_type=F32)


def chunk_column(step, z):
    far = (step + 1) // 2
    return jnp.where(step % 2 == 1, z - far + 8, z + far) % 8


def layer_kernel(
    tok_ref, idx_ref, logit_ref, ten_ref, adp_ref, win_ref, wout_ref, fin_ref, fup_ref, out_ref,
    tokbuf, meta, sel, mix, xsend, xrecv, code_s, code_r, winb, woutb, finb, fupb, wide, pre, act,
    xret, part, rs_s, rs_r,
    y_ss, y_rs, m_ss, m_rs, x_ss, x_rs, c_ss, c_rs, w_ss, w_rs, b_ss, b_rs, r_ss, r_rs,
):
    toks = tok_ref.shape[0]
    topk = idx_ref.shape[0]
    width = tok_ref.shape[1] // CHUNKS
    hidden = wout_ref.shape[0]
    rank = fin_ref.shape[0]
    block = NY * SLOTS
    half = toks // 2
    e = lax.axis_index("expert")
    z = lax.axis_index("store")
    x, y, c = e // (NY * NC), (e // NC) % NY, e % NC

    def at(dx, dy, dc):
        return (((x + dx) % NX * NY + (y + dy) % NY) * NC + (c + dc) % NC, z)

    def away(p):
        return at(p // NC, 0, p % NC)

    def back(p):
        return at(NX - p // NC, 0, p % NC)

    ring = (at(0, 1, 0), at(0, NY - 1, 0))
    zring = ((e, (z + 1) % 8), (e, (z + 7) % 8))

    def remote(src, dst, ss, rs, dev):
        return pltpu.make_async_remote_copy(
            src_ref=src, dst_ref=dst, send_sem=ss, recv_sem=rs, device_id=dev, device_id_type=MESH
        )

    barrier = pltpu.get_barrier_semaphore()
    partners = [*ring, *zring] + [away(p) for p in range(1, PEERS)]
    for dev in partners:
        pl.semaphore_signal(barrier, inc=1, device_id=dev, device_id_type=MESH)

    winb[z] = win_ref[...]
    woutb[z] = wout_ref[...]
    fupb[z] = fup_ref[...]
    for k in range(CHUNKS):
        finb[z, k] = fin_ref[:, k * width : (k + 1) * width]

    def take(k, _):
        col = pl.multiple_of(chunk_column(k, z) * width, width)
        tokbuf[k, 0] = tok_ref[:, pl.ds(col, width)]
        return 0

    lax.fori_loop(0, CHUNKS, take, 0)

    ids = idx_ref[...]
    experts = NX * NY * NC
    named = lax.broadcasted_iota(jnp.int32, (experts, toks), 0)
    chosen = jnp.zeros((experts, toks), F32)
    for k in range(topk):
        chosen = chosen + jnp.where(ids[k : k + 1, :] == named, 1.0, 0.0)
    before = jnp.where(
        lax.broadcasted_iota(jnp.int32, (toks, toks), 0)
        < lax.broadcasted_iota(jnp.int32, (toks, toks), 1),
        1.0,
        0.0,
    ).astype(BF16)
    rank_of = dot(chosen.astype(BF16), before)
    peer = (((ids // (NY * NC)) - x + NX) % NX) * NC + (ids % NC + c) % NC
    place = ((ids // NC) % NY * 256 + peer * 32).astype(F32)
    for k in range(topk):
        slot = jnp.sum(jnp.where(ids[k : k + 1, :] == named, rank_of, 0.0), axis=0, keepdims=True)
        meta[0, k : k + 1, :] = place[k : k + 1, :] + slot
    logits = logit_ref[...]
    meta[0, topk : 2 * topk, :] = logits / jnp.sum(logits, axis=0, keepdims=True)
    meta[0, 2 * topk : 3 * topk, :] = jnp.broadcast_to(ten_ref[...], (topk, toks)).astype(F32)

    pl.semaphore_wait(barrier, len(partners))

    def zcopies(kind, h):
        out = []
        for d in range(2):
            src_z = (z - (h - 1) + 8) % 8 if d == 0 else (z + (h - 1)) % 8
            ss, rs = w_ss.at[kind, h - 1, d], w_rs.at[kind, h - 1, d]
            ref = (finb, fupb, winb, woutb)[kind].at[src_z]
            if h == 4:
                n = ref.shape[0] // 2
                ref = ref.at[pl.ds(d * n, n)]
            out.append((ref, ss, rs, d))
        return out

    def zsend(kind, h):
        for ref, ss, rs, d in zcopies(kind, h):
            remote(ref, ref, ss, rs, zring[d]).start()

    def zarrive(kind, h):
        for ref, ss, rs, d in zcopies(kind, h):
            remote(ref, ref, ss, rs, zring[d]).wait_recv()

    def zsent(kind, h):
        for ref, ss, rs, d in zcopies(kind, h):
            remote(ref, ref, ss, rs, zring[d]).wait_send()

    def place_of(h, d):
        return 0 if h == 0 else (7 if h == 4 else 2 * h - 1 + d)

    def ycopy(k, h, d):
        src, dst = tokbuf.at[k, place_of(h - 1, d)], tokbuf.at[k, place_of(h, d)]
        if h == 4:
            src, dst = src.at[pl.ds(d * half, half)], dst.at[pl.ds(d * half, half)]
        return remote(src, dst, y_ss.at[k, h - 1, d], y_rs.at[k, h - 1, d], ring[d])

    def mcopy(h, d):
        src, dst = meta.at[place_of(h - 1, d)], meta.at[place_of(h, d)]
        return remote(src, dst, m_ss.at[h - 1, d], m_rs.at[h - 1, d], ring[d])

    def hops_of_meta(h):
        return (0,) if h == 4 else (0, 1)

    row_no = lax.broadcasted_iota(jnp.int32, (256, toks), 0)

    def build(q):
        want = (row_no + (y * 256 - 2 * q)).astype(F32)
        hot = jnp.zeros((256, toks), F32)
        share = jnp.zeros((256, toks), F32)
        for k in range(topk):
            same = meta[q, k : k + 1, :] == want
            hot = jnp.where(same, 1.0, hot)
            share = jnp.where(same, meta[q, topk + k : topk + k + 1, :], share)
        hot = hot.astype(BF16).reshape(PEERS, 2, TILE, toks)
        sel[q, :, toks : 2 * toks] = hot[:, 0].reshape(PEERS * TILE, toks)
        sel[q + 1, :, 0:toks] = hot[:, 1].reshape(PEERS * TILE, toks)
        share = share.T
        high = share.astype(BF16)
        mix[q, 0:toks] = high
        mix[q, toks : 2 * toks] = (share - high.astype(F32)).astype(BF16)

    def tenants():
        lane_of = lax.broadcasted_iota(jnp.int32, (TILE, toks), 0)
        codes = jnp.zeros((TILE, PEERS * TILE), F32)
        for i in range(NY + 1):
            mine = lane_of == i
            if i > 0:
                v = jnp.where(mine, meta[i - 1, 2 * topk : 2 * topk + 1, :], 0.0).astype(BF16)
                codes = codes + dot(v, sel[i, :, 0:toks], ((1,), (1,)))
            if i < NY:
                v = jnp.where(mine, meta[i, 2 * topk : 2 * topk + 1, :], 0.0).astype(BF16)
                codes = codes + dot(v, sel[i, :, toks : 2 * toks], ((1,), (1,)))
        code_s[...] = codes.astype(BF16)
        code_r[0] = codes.astype(BF16)

    def ccopy(p):
        return remote(code_s, code_r.at[p], c_ss.at[p - 1], c_rs.at[p - 1], away(p))

    def xcopy(k, p):
        return remote(
            xsend.at[k, p - 1], xrecv.at[k, p], x_ss.at[k, p - 1], x_rs.at[k, p - 1], away(p)
        )

    def select(k):
        for i in range(NY + 1):
            if i == 0:
                rows = dot(sel[0, :, toks : 2 * toks], tokbuf[k, 0])
            elif i == NY:
                rows = dot(sel[NY, :, 0:toks], tokbuf[k, NY - 1])
            else:
                rows = dot(sel[i], tokbuf[k, i - 1 : i + 1].reshape(2 * toks, width))
            rows = rows.astype(BF16).reshape(PEERS, TILE, width)
            xrecv[k, 0, i * TILE : (i + 1) * TILE] = rows[0]
            xsend[k, :, i * TILE : (i + 1) * TILE] = rows[1:]

    order = [4, 5, 2, 3, 6, 7, 1]

    def accumulate(k):
        col = chunk_column(k, z)
        for p in range(1, PEERS):
            xcopy(k, p).wait_recv()

        def group(g, _):
            rows = xrecv[k, pl.ds(g * GROUP, GROUP)].reshape(GROUP * block, width)
            weight = winb[col]
            factor = finb[:, col].reshape(8 * rank, width)
            pre[g, :, 0 : 2 * hidden] += dot(rows, weight)
            pre[g, :, 2 * hidden :] += dot(rows, factor, ((1,), (1,)))
            return 0

        lax.fori_loop(0, PEERS // GROUP, group, 0)

    zsend(0, 1)
    zsend(1, 1)
    pre[...] = jnp.zeros_like(pre)

    def slot_a(t, _):
        for h in range(4, 0, -1):
            k = t - h

            @pl.when((k >= 0) & (k < CHUNKS))
            def _():
                for d in range(2):
                    ycopy(k, h, d).wait_recv()
                    if h < 4:
                        ycopy(k, h + 1, d).start()

            @pl.when(k == 0)
            def _():
                for d in hops_of_meta(h):
                    mcopy(h, d).wait_recv()
                if h < 4:
                    for d in hops_of_meta(h + 1):
                        mcopy(h + 1, d).start()

        @pl.when(t == 0)
        def _():
            for d in range(2):
                mcopy(1, d).start()

        @pl.when(t < CHUNKS)
        def _():
            for d in range(2):
                ycopy(t, 1, d).start()

        for h in range(0, 5):

            @pl.when(t == h)
            def _():
                for q in range(max(0, 2 * h - 1), min(2 * h, 7) + 1):
                    build(q)

        @pl.when(t == 4)
        def _():
            tenants()
            for p in order:
                ccopy(p).start()

        @pl.when((t >= 4) & (t < CHUNKS + 4))
        def _():
            k = t - 4
            select(k)
            for p in order:
                xcopy(k, p).start()

        for h in range(1, 5):

            @pl.when(t == h)
            def _():
                for kind in (0, 1):
                    zarrive(kind, h)
                    if h < 4:
                        zsend(kind, h + 1)
                if h == 1:
                    zsend(2, 1)

            @pl.when(t == Z_IN[h - 1])
            def _():
                zarrive(2, h)
                if h < 4:
                    zsend(2, h + 1)
                else:
                    zsend(3, 1)

        for h in range(1, 4):

            @pl.when(t == Z_OUT[h - 1])
            def _():
                zarrive(3, h)
                zsend(3, h + 1)

        @pl.when(t >= 5)
        def _():
            accumulate(t - 5)

        return 0

    lax.fori_loop(0, CHUNKS + 5, slot_a, 0)

    for u in range(8):
        r = u * rank
        wide[r : r + rank // 2, 0:hidden] = fupb[u, 0 : rank // 2]
        wide[r : r + rank // 2, hidden:] = jnp.zeros((rank // 2, hidden), BF16)
        wide[r + rank // 2 : r + rank, 0:hidden] = jnp.zeros((rank // 2, hidden), BF16)
        wide[r + rank // 2 : r + rank, hidden:] = fupb[u, rank // 2 :]
    for p in range(1, PEERS):
        ccopy(p).wait_recv()

    def activate(p, _):
        g, b = p // GROUP, (p % GROUP) * block
        rows = pl.ds(pl.multiple_of(b, block), block)
        codes = code_r[p].astype(F32)
        lane = lax.broadcasted_iota(jnp.int32, (TILE, PEERS * TILE), 1)
        mine = lane == p * TILE + lax.broadcasted_iota(jnp.int32, (TILE, PEERS * TILE), 0)
        column = jnp.concatenate(
            [
                jnp.sum(jnp.where(mine, codes[i : i + 1, :], 0.0), axis=1, keepdims=True)
                for i in range(NY + 1)
            ],
            axis=0,
        )
        of_lane = (lax.broadcasted_iota(jnp.int32, (block, 8 * rank), 1) // rank).astype(F32)
        keep = jnp.where(column == of_lane, adp_ref[...], 0.0)
        low = (pre[g, rows, 2 * hidden :] * keep).astype(BF16)
        total = pre[g, rows, 0 : 2 * hidden] + dot(low, wide[...])
        gate, up = total[:, :hidden], total[:, hidden:]
        act[g, rows] = (gate / (1.0 + jnp.exp(-gate)) * up).astype(BF16)
        return 0

    lax.fori_loop(0, PEERS, activate, 0)

    def sent(k, _):
        for p in range(1, PEERS):
            xcopy(k, p).wait_send()
        for h in range(1, 5):
            for d in range(2):
                ycopy(k, h, d).wait_send()
        return 0

    lax.fori_loop(0, CHUNKS, sent, 0)
    for p in range(1, PEERS):
        ccopy(p).wait_send()
    for h in range(1, 5):
        for d in hops_of_meta(h):
            mcopy(h, d).wait_send()
    zarrive(3, 4)

    def bcopy(k, p):
        return remote(
            xsend.at[k, p - 1], xret.at[k, p], b_ss.at[k, p - 1], b_rs.at[k, p - 1], back(p)
        )

    def rcopy(k, h, d):
        src, dst = rs_s.at[k, h - 1, d], rs_r.at[k, h - 1, d]
        if h == 4:
            src, dst = src.at[pl.ds(d * half, half)], dst.at[pl.ds(d * half, half)]
        return remote(src, dst, r_ss.at[k, h - 1, d], r_rs.at[k, h - 1, d], ring[1 - d])

    def down(k):
        col = chunk_column(k, z)
        for g in (1, 0):
            rows = dot(act[g], woutb[col]).astype(BF16).reshape(GROUP, block, width)
            if g == 0:
                xret[k, 0] = rows[0]
                xsend[k, 0 : GROUP - 1] = rows[1:]
            else:
                xsend[k, GROUP - 1 : 2 * GROUP - 1] = rows
            for p in order:
                if p // GROUP == g:
                    bcopy(k, p).start()

    def combine(k):
        for p in range(1, PEERS):
            bcopy(k, p).wait_recv()
        for q in range(NY - 1, -1, -1):
            rows = xret[k, :, q * TILE : (q + 2) * TILE].reshape(256, width)
            both = dot(mix[q], rows)
            total = both[:toks] + both[toks:]
            if q == NY - 1:
                for d in range(2):
                    rs_s[k, 3, d, d * half : (d + 1) * half] = total[d * half : (d + 1) * half].astype(BF16)
                    rcopy(k, 4, d).start()
            else:
                part[k, q] = total

    def slot_b(t, _):
        for h in range(1, 5):
            k = t - 1 - (5 - h)

            @pl.when((k >= 0) & (k < CHUNKS))
            def _():
                for d in range(2):
                    rcopy(k, h, d).wait_recv()
                    if h == 1:
                        continue
                    q = place_of(h - 1, d)
                    span = slice(d * half, (d + 1) * half)
                    if h == 4:
                        rest = slice((1 - d) * half, (2 - d) * half)
                        rs_s[k, h - 2, d, rest] = part[k, q, rest].astype(BF16)
                    else:
                        span = slice(0, toks)
                    rs_s[k, h - 2, d, span] = (
                        part[k, q, span] + rs_r[k, h - 1, d, span].astype(F32)
                    ).astype(BF16)
                    rcopy(k, h - 1, d).start()
                if h == 1:
                    total = part[k, 0] + rs_r[k, 0, 0].astype(F32) + rs_r[k, 0, 1].astype(F32)
                    col = pl.multiple_of(chunk_column(k, z) * width, width)
                    out_ref[:, pl.ds(col, width)] = total.astype(BF16)

        @pl.when(t < CHUNKS)
        def _():
            down(t)

        @pl.when((t >= 1) & (t < CHUNKS + 1))
        def _():
            combine(t - 1)

        return 0

    lax.fori_loop(0, CHUNKS + 5, slot_b, 0)

    def drained(k, _):
        for p in range(1, PEERS):
            bcopy(k, p).wait_send()
        for h in range(1, 5):
            for d in range(2):
                rcopy(k, h, d).wait_send()
        return 0

    lax.fori_loop(0, CHUNKS, drained, 0)
    for kind in range(4):
        for h in range(1, 5):
            zsent(kind, h)


Z_IN = (3, 5, 7, 8)
Z_OUT = (9, 10, 11)


def shards(
    tokens,
    chosen_expert_index,
    router_weight_logits,
    token_tenant_index,
    adapted,
    gate_up_weight,
    down_weight,
    adapter_input_factors,
    adapter_output_factors,
):
    toks, model = tokens.shape
    width = model // CHUNKS
    hidden = down_weight.shape[1]
    rank = adapter_input_factors.shape[2]
    block = NY * SLOTS
    kept = jnp.repeat(adapted[:, 0].astype(F32), rank)[None, :]
    vmem = pl.BlockSpec(memory_space=pltpu.VMEM)
    dma = pltpu.SemaphoreType.DMA
    return pl.pallas_call(
        layer_kernel,
        out_shape=jax.ShapeDtypeStruct((toks, model), BF16),
        in_specs=[vmem] * 9,
        out_specs=vmem,
        scratch_shapes=[
            pltpu.VMEM((CHUNKS, NY, toks, width), BF16),
            pltpu.VMEM((NY, 24, toks), F32),
            pltpu.VMEM((NY + 1, PEERS * TILE, 2 * toks), BF16),
            pltpu.VMEM((NY, 2 * toks, 256), BF16),
            pltpu.VMEM((CHUNKS, PEERS - 1, block, width), BF16),
            pltpu.VMEM((CHUNKS, PEERS, block, width), BF16),
            pltpu.VMEM((TILE, PEERS * TILE), BF16),
            pltpu.VMEM((PEERS, TILE, PEERS * TILE), BF16),
            pltpu.VMEM((8, width, 2 * hidden), BF16),
            pltpu.VMEM((8, hidden, width), BF16),
            pltpu.VMEM((8, CHUNKS, rank, width), BF16),
            pltpu.VMEM((8, rank, hidden), BF16),
            pltpu.VMEM((8 * rank, 2 * hidden), BF16),
            pltpu.VMEM((PEERS // GROUP, GROUP * block, 2 * hidden + 8 * rank), F32),
            pltpu.VMEM((PEERS // GROUP, GROUP * block, hidden), BF16),
            pltpu.VMEM((CHUNKS, PEERS, block, width), BF16),
            pltpu.VMEM((CHUNKS, NY - 1, toks, width), F32),
            pltpu.VMEM((CHUNKS, 4, 2, toks, width), BF16),
            pltpu.VMEM((CHUNKS, 4, 2, toks, width), BF16),
            dma((CHUNKS, 4, 2)),
            dma((CHUNKS, 4, 2)),
            dma((4, 2)),
            dma((4, 2)),
            dma((CHUNKS, PEERS - 1)),
            dma((CHUNKS, PEERS - 1)),
            dma((PEERS - 1,)),
            dma((PEERS - 1,)),
            dma((4, 4, 2)),
            dma((4, 4, 2)),
            dma((CHUNKS, PEERS - 1)),
            dma((CHUNKS, PEERS - 1)),
            dma((CHUNKS, 4, 2)),
            dma((CHUNKS, 4, 2)),
        ],
        compiler_params=pltpu.CompilerParams(
            collective_id=0, has_side_effects=True, vmem_limit_bytes=60 * 1024 * 1024
        ),
        cost_estimate=pl.CostEstimate(flops=8 * 10**9, bytes_accessed=3 * 10**6, transcendentals=0),
    )(
        tokens,
        chosen_expert_index.T,
        router_weight_logits.T,
        token_tenant_index[None, :],
        kept,
        gate_up_weight[0],
        down_weight[0],
        adapter_input_factors[0, 0],
        adapter_output_factors[0, 0],
    )


def solution(mesh):
    placed = (
        P(("expert", "store"), None),
        P(("expert", "store"), None),
        P(("expert", "store"), None),
        P(("expert", "store")),
        P(None, "expert"),
        P("expert", "store", None),
        P("expert", None, "store"),
        P("store", "expert", None, None),
        P("store", "expert", None, None),
    )
    return jax.shard_map(
        shards, mesh=mesh, in_specs=placed, out_specs=P(("expert", "store"), None), check_vma=False
    )
```

time: 445 us -> 177 us (0.40)
  waiting for transfers between devices: 279 us -> 0 us
  Pallas kernels: 0 us -> 173 us
  local copies, waits for them, and re-layouts: 71.3 us -> 3.25 us
  starting transfers between devices: 28.7 us -> 0 us
  other arithmetic: 27.9 us -> 0.01 us
  matrix products: 23.8 us -> 0 us
  between operations: 13.3 us -> 0.01 us
    all_to_all x3 -> x0, waiting for transfers between devices: 235 us -> none  [the longest x1 141 us: shards(): lax.all_to_all(expert_out.reshape(sources, slot_count, model_width), 'exp...]
    pallas_call x0 -> x1, Pallas kernels: none -> 173 us  [shards(): pl.pallas_call(layer_kernel, out_shape=jax.ShapeDtypeStruct((toks, model)...]
    all_gather x3 -> x0, waiting for transfers between devices: 43.4 us -> none  [the longest x1 43.4 us: in_one_piece(): result = lax.all_gather(both, axis, axis=dim, tiled=True)]
    reshape x5 -> x0, local copies, waits for them, and re-layouts: 38.4 us -> none  [the longest x2 15.6 us: shards(): flat_rows = row_block.reshape(-1, model_width)]
    all_to_all x3 -> x0, starting transfers between devices: 28.4 us -> none  [the longest x1 11.6 us: shards(): lax.all_to_all(send_codes, 'expert', split_axis=0, concat_axis=0, tiled=T...]
    gather x3 -> x0, local copies, waits for them, and re-layouts: 24.9 us -> none  [the longest x1 11.8 us: shards(): returned.reshape(-1, model_width)[slot_of]]
    dot_general x3 -> x0, matrix products: 23.8 us -> none  [the longest x1 9.92 us: shards(): jnp.dot(flat_rows, weight_in[0], preferred_element_type=jnp.float32)]
    another operation x2 -> x0, other arithmetic: 18 us -> none
  transfers between devices with their start and end apart: 6 -> 0, of which waited for: 3 -> 0; matrix products, arithmetic and copies ran while one was open for 11% -> 0% of each run, Pallas kernels for 0% -> 0%
where the time goes in v1:
time: 177 us; the launch traced here: 176 us
  Pallas kernels  173 us (98%)
  local copies, waits for them, and re-layouts  3.25 us (2%)
    pallas_call x1, Pallas kernels, shards(): pl.pallas_call(layer_kernel, out_shape=jax.ShapeDtypeStruct((toks, model)...  173 us

profile of v1, /device:TPU:1, one launch (start us, length us, event | category | flops | bytes accessed | tf_op | source)
XLA Modules:
  0.0 176.1 jit_solution(17705255816143812806)
XLA Ops:
  0.0 0.0 copy-start
  0.0 0.7 copy-done
  0.7 0.1 broadcast_in_dim.7
  0.7 0.6 broadcast_in_dim_reshape.3.adp_ref
  1.4 172.9 %shard_map.91 = bf16[128,2048]{1,0:T(8,128)(2,1)} custom-call(bf16[128,2048]{1,0:T(8,128)(2,1)} %tok_ref.1, s32[8,128]{1,0:T(8,128)} %bitcast.13, f32[8,128]{1,0:T(8,128)} %bitcast.14, s32[1,128]{1,0:T(1,128)} %bitcast.15, f32[1,256]{1,0:T(1,128)} %broadcast_in_dim_reshape.3.adp_ref, bf16[256,768]{1,0:T(8,128)(2,1)} %bitcast.9, bf16[384,256]{1,0:T(8,128)(2,1)} %bitcast.10, ...), custom_call_target="tpu_custom_call" | custom-call | flops 8000000000 | bytes 3000000 | tf_op jit(solution)/shard_map/pallas_call | solution.py:462
  174.2 1.9 %copy.11 = bf16[128,2048]{1,0:T(8,128)(2,1)} copy(bf16[128,2048]{1,0:T(8,128)(2,1)} %shard_map.91) | data formatting | bytes 1048576
  (1 shorter events, 0.0 us)
Async XLA Ops:
  0.0 0.7 copy-start

commit v2 on v1

v2 whole, which is shorter than its diff:
```python
import jax
import jax.numpy as jnp
from jax import lax
from jax.experimental import pallas as pl
from jax.experimental.pallas import tpu as pltpu
from jax.sharding import PartitionSpec as P

MESH = pl.DeviceIdType.MESH
NX, NY, NC = 4, 8, 2
PEERS = NX * NC
SLOTS = 18
TILE = 16
CHUNKS = 8
GROUP = 4
LAG = 2
F32, BF16 = jnp.float32, jnp.bfloat16


def dot(a, b, dims=((1,), (0,))):
    return lax.dot_general(a, b, (dims, ((), ())), preferred_element_type=F32)


def chunk_column(step, z):
    far = (step + 1) // 2
    return jnp.where(step % 2 == 1, z - far + 8, z + far) % 8


def layer_kernel(
    tok_ref, idx_ref, logit_ref, ten_ref, adp_ref, win_ref, wout_ref, fin_ref, fup_ref, out_ref,
    tokbuf, meta, sel, mix, xsend, xrecv, code_s, code_r, winb, woutb, finb, fupb, wide, pre, act,
    xret, own, rs_s, rs_r,
    y_ss, y_rs, m_ss, m_rs, x_ss, x_rs, c_ss, c_rs, w_ss, w_rs, b_ss, b_rs, r_ss, r_rs,
):
    toks = tok_ref.shape[0]
    topk = idx_ref.shape[0]
    width = tok_ref.shape[1] // CHUNKS
    hidden = wout_ref.shape[0]
    rank = fin_ref.shape[0]
    block = NY * SLOTS
    half = toks // 2
    e = lax.axis_index("expert")
    z = lax.axis_index("store")
    x, y, c = e // (NY * NC), (e // NC) % NY, e % NC

    def at(dx, dy, dc):
        return (((x + dx) % NX * NY + (y + dy) % NY) * NC + (c + dc) % NC, z)

    def away(p):
        return at(p // NC, 0, p % NC)

    def back(p):
        return at(NX - p // NC, 0, p % NC)

    ring = (at(0, 1, 0), at(0, NY - 1, 0))
    zring = ((e, (z + 1) % 8), (e, (z + 7) % 8))

    def remote(src, dst, ss, rs, dev):
        return pltpu.make_async_remote_copy(
            src_ref=src, dst_ref=dst, send_sem=ss, recv_sem=rs, device_id=dev, device_id_type=MESH
        )

    def await_bytes(ref, sem):
        pltpu.make_async_copy(ref, ref, sem).wait()

    barrier = pltpu.get_barrier_semaphore()
    partners = [*ring, *zring] + [away(p) for p in range(1, PEERS)]
    for dev in partners:
        pl.semaphore_signal(barrier, inc=1, device_id=dev, device_id_type=MESH)

    winb[z] = win_ref[...]
    woutb[z] = wout_ref[...]
    fupb[z] = fup_ref[...]
    for k in range(CHUNKS):
        finb[z, k] = fin_ref[:, k * width : (k + 1) * width]

    def take(k, _):
        col = pl.multiple_of(chunk_column(k, z) * width, width)
        tokbuf[k, 0] = tok_ref[:, pl.ds(col, width)]
        return 0

    lax.fori_loop(0, CHUNKS, take, 0)

    ids = idx_ref[...]
    experts = NX * NY * NC
    named = lax.broadcasted_iota(jnp.int32, (experts, toks), 0)
    chosen = jnp.zeros((experts, toks), F32)
    for k in range(topk):
        chosen = chosen + jnp.where(ids[k : k + 1, :] == named, 1.0, 0.0)
    before = jnp.where(
        lax.broadcasted_iota(jnp.int32, (toks, toks), 0)
        < lax.broadcasted_iota(jnp.int32, (toks, toks), 1),
        1.0,
        0.0,
    ).astype(BF16)
    rank_of = dot(chosen.astype(BF16), before)
    peer = (((ids // (NY * NC)) - x + NX) % NX) * NC + (ids % NC + c) % NC
    place = ((ids // NC) % NY * 256 + peer * 32).astype(F32)
    for k in range(topk):
        slot = jnp.sum(jnp.where(ids[k : k + 1, :] == named, rank_of, 0.0), axis=0, keepdims=True)
        meta[0, k : k + 1, :] = place[k : k + 1, :] + slot
    logits = logit_ref[...]
    meta[0, topk : 2 * topk, :] = logits / jnp.sum(logits, axis=0, keepdims=True)
    meta[0, 2 * topk : 3 * topk, :] = jnp.broadcast_to(ten_ref[...], (topk, toks)).astype(F32)

    pl.semaphore_wait(barrier, len(partners))

    kinds = (finb, fupb, winb, woutb)
    FIN, FUP, WIN, WOUT = range(4)

    def zsend(kind, h):
        for d in range(2):
            ref = kinds[kind].at[(z - (h - 1) + 8) % 8 if d == 0 else (z + (h - 1)) % 8]
            if h == 4:
                n = ref.shape[0] // 2
                ref = ref.at[pl.ds(d * n, n)]
            remote(ref, ref, w_ss.at[kind], w_rs.at[kind, h - 1], zring[d]).start()

    def zarrive(kind, h):
        await_bytes(kinds[kind].at[pl.ds(0, 1 if h == 4 else 2)], w_rs.at[kind, h - 1])

    def place_of(h, d):
        return 0 if h == 0 else (7 if h == 4 else 2 * h - 1 + d)

    def ysend(k, h):
        for d in range(2):
            src, dst = tokbuf.at[k, place_of(h - 1, d)], tokbuf.at[k, place_of(h, d)]
            if h == 4:
                src, dst = src.at[pl.ds(d * half, half)], dst.at[pl.ds(d * half, half)]
            remote(src, dst, y_ss.at[h // 4], y_rs.at[k, h - 1], ring[d]).start()

    def yarrive(k, h):
        await_bytes(tokbuf.at[k, pl.ds(0, 1 if h == 4 else 2)], y_rs.at[k, h - 1])

    def msend(h):
        for d in range(1 if h == 4 else 2):
            remote(meta.at[place_of(h - 1, d)], meta.at[place_of(h, d)], m_ss, m_rs.at[h - 1], ring[d]).start()

    def marrive(h):
        await_bytes(meta.at[pl.ds(0, 1 if h == 4 else 2)], m_rs.at[h - 1])

    row_no = lax.broadcasted_iota(jnp.int32, (256, toks), 0)

    def build(q):
        want = (row_no + (y * 256 - 2 * q)).astype(F32)
        hot = jnp.zeros((256, toks), F32)
        share = jnp.zeros((256, toks), F32)
        for k in range(topk):
            same = meta[q, k : k + 1, :] == want
            hot = jnp.where(same, 1.0, hot)
            share = jnp.where(same, meta[q, topk + k : topk + k + 1, :], share)
        hot = hot.astype(BF16).reshape(PEERS, 2, TILE, toks)
        sel[q, :, toks : 2 * toks] = hot[:, 0].reshape(PEERS * TILE, toks)
        sel[q + 1, :, 0:toks] = hot[:, 1].reshape(PEERS * TILE, toks)
        share = share.T
        high = share.astype(BF16)
        mix[q, 0:toks] = high
        mix[q, toks : 2 * toks] = (share - high.astype(F32)).astype(BF16)

    def tenants():
        lane_of = lax.broadcasted_iota(jnp.int32, (TILE, toks), 0)
        codes = jnp.zeros((TILE, PEERS * TILE), F32)
        for i in range(NY + 1):
            mine = lane_of == i
            if i > 0:
                v = jnp.where(mine, meta[i - 1, 2 * topk : 2 * topk + 1, :], 0.0).astype(BF16)
                codes = codes + dot(v, sel[i, :, 0:toks], ((1,), (1,)))
            if i < NY:
                v = jnp.where(mine, meta[i, 2 * topk : 2 * topk + 1, :], 0.0).astype(BF16)
                codes = codes + dot(v, sel[i, :, toks : 2 * toks], ((1,), (1,)))
        code_s[...] = codes.astype(BF16)
        code_r[0] = codes.astype(BF16)

    order = [4, 5, 2, 3, 6, 7, 1]
    tiles = {h: (0 if h == 1 else 2 * h - 1, 2 * h + 1) for h in range(1, 5)}

    def rows_of(h):
        return pl.ds(tiles[h][0] * TILE, (tiles[h][1] - tiles[h][0]) * TILE)

    def select(k, h):
        for i in range(*tiles[h]):
            if i == 0:
                rows = dot(sel[0, :, toks : 2 * toks], tokbuf[k, 0])
            elif i == NY:
                rows = dot(sel[NY, :, 0:toks], tokbuf[k, NY - 1])
            else:
                rows = dot(sel[i], tokbuf[k, i - 1 : i + 1].reshape(2 * toks, width))
            rows = rows.astype(BF16).reshape(PEERS, TILE, width)
            xrecv[k, 0, i * TILE : (i + 1) * TILE] = rows[0]
            xsend[k, 1:, i * TILE : (i + 1) * TILE] = rows[1:]
        for p in order:
            remote(
                xsend.at[k, p, rows_of(h)], xrecv.at[k, p, rows_of(h)], x_ss, x_rs.at[k], away(p)
            ).start()

    def xarrive(k):
        await_bytes(xrecv.at[k, pl.ds(1, PEERS - 1)], x_rs.at[k])

    def block_rows(k, g):
        return xrecv[k, pl.ds(g * GROUP, GROUP)].reshape(GROUP * block, width)

    def accumulate(k, g):
        pre[g, :, 0 : 2 * hidden] += dot(block_rows(k, g), winb[chunk_column(k, z)])

    def lower(k, g):
        factor = finb[:, chunk_column(k, z)].reshape(8 * rank, width)
        pre[g, :, 2 * hidden :] += dot(block_rows(k, g), factor, ((1,), (1,)))

    def lower_of(first, last):
        def step(i, _):
            lower(i // 2, i % 2)
            return 0

        lax.fori_loop(2 * first, 2 * last, step, 0)

    for kind in (WIN, FIN, FUP):
        zsend(kind, 1)
    pre[...] = jnp.zeros_like(pre)

    def slot_a(t, _):
        for h in range(4, 0, -1):
            k = t - h

            @pl.when((k >= 0) & (k < CHUNKS))
            def _():
                yarrive(k, h)
                if h < 4:
                    ysend(k, h + 1)

            @pl.when(k == 0)
            def _():
                marrive(h)
                if h < 4:
                    msend(h + 1)

        @pl.when(t == 0)
        def _():
            msend(1)

        @pl.when(t < CHUNKS)
        def _():
            ysend(t, 1)

        for h in range(0, 5):

            @pl.when(t == h)
            def _():
                for q in range(max(0, 2 * h - 1), min(2 * h, 7) + 1):
                    build(q)

        for h in range(4, 0, -1):
            k = t - h

            @pl.when((k >= 0) & (k < CHUNKS))
            def _():
                select(k, h)

        @pl.when(t == 4)
        def _():
            tenants()
            for p in order:
                remote(code_s, code_r.at[p], c_ss, c_rs, away(p)).start()
            for kind in (WIN, FIN, FUP):
                zarrive(kind, 1)
                zsend(kind, 2)

        @pl.when(t == 6)
        def _():
            zarrive(WIN, 2)
            zsend(WIN, 3)

        @pl.when(t == 7)
        def _():
            for kind in (FIN, FUP):
                zarrive(kind, 2)
                zsend(kind, 3)

        @pl.when(t == 8)
        def _():
            zarrive(WIN, 3)
            zsend(WIN, 4)

        @pl.when(t == 9)
        def _():
            for kind in (FIN, FUP):
                zarrive(kind, 3)
                zsend(kind, 4)

        @pl.when(t == 10)
        def _():
            zarrive(WIN, 4)
            zsend(WOUT, 1)
            for kind in (FIN, FUP):
                zarrive(kind, 4)
            lower_of(0, 4)

        @pl.when(t == 11)
        def _():
            lower_of(4, 6)

        @pl.when(t >= 5)
        def _():
            xarrive(t - 5)

            def group(g, _):
                accumulate(t - 5, g)
                return 0

            lax.fori_loop(0, PEERS // GROUP, group, 0)

        return 0

    lax.fori_loop(0, CHUNKS + 4, slot_a, 0)

    for u in range(8):
        r = u * rank
        wide[r : r + rank // 2, 0:hidden] = fupb[u, 0 : rank // 2]
        wide[r : r + rank // 2, hidden:] = jnp.zeros((rank // 2, hidden), BF16)
        wide[r + rank // 2 : r + rank, 0:hidden] = jnp.zeros((rank // 2, hidden), BF16)
        wide[r + rank // 2 : r + rank, hidden:] = fupb[u, rank // 2 :]
    lower_of(6, 7)
    await_bytes(code_r.at[pl.ds(1, PEERS - 1)], c_rs)
    lane_rank = lax.broadcasted_iota(jnp.int32, (1, 8 * rank), 1) // rank
    adapted = jnp.zeros((1, 8 * rank), F32)
    for u in range(8):
        adapted = jnp.where(lane_rank == u, adp_ref[0, u].astype(F32), adapted)

    def activate(p):
        g, b = p // GROUP, (p % GROUP) * block
        rows = pl.ds(pl.multiple_of(b, block), block)
        codes = code_r[p].astype(F32)
        lane = lax.broadcasted_iota(jnp.int32, (TILE, PEERS * TILE), 1)
        mine = lane == p * TILE + lax.broadcasted_iota(jnp.int32, (TILE, PEERS * TILE), 0)
        column = jnp.concatenate(
            [
                jnp.sum(jnp.where(mine, codes[i : i + 1, :], 0.0), axis=1, keepdims=True)
                for i in range(NY + 1)
            ],
            axis=0,
        )
        of_lane = (lax.broadcasted_iota(jnp.int32, (block, 8 * rank), 1) // rank).astype(F32)
        keep = jnp.where(column == of_lane, adapted, 0.0)
        low = (pre[g, rows, 2 * hidden :] * keep).astype(BF16)
        total = pre[g, rows, 0 : 2 * hidden] + dot(low, wide[...])
        gate, up = total[:, :hidden], total[:, hidden:]
        act[g, rows] = (gate / (1.0 + jnp.exp(-gate)) * up).astype(BF16)

    await_bytes(xsend.at[:, pl.ds(1, PEERS - 1)], x_ss)

    def send_back(k, h, p):
        remote(
            xsend.at[k, p, rows_of(h)], xret.at[k, p, rows_of(h)], b_ss, b_rs.at[k, h - 1], back(p)
        ).start()

    def returned(k, h):
        await_bytes(xret.at[k, pl.ds(1, PEERS - 1), rows_of(h)], b_rs.at[k, h - 1])

    def rsend(k, h, d):
        src, dst = rs_s.at[k, h - 1, d], rs_r.at[k, h - 1, d]
        if h == 4:
            src, dst = src.at[pl.ds(d * half, half)], dst.at[pl.ds(d * half, half)]
        remote(src, dst, r_ss.at[h // 4], r_rs.at[k, h - 1], ring[1 - d]).start()

    def rarrive(k, h):
        await_bytes(rs_r.at[k, h - 1, pl.ds(0, 1 if h == 4 else 2)], r_rs.at[k, h - 1])

    def down(k, g):
        rows = dot(act[g], woutb[chunk_column(k, z)]).astype(BF16).reshape(GROUP, block, width)
        xsend[k, pl.ds(g * GROUP, GROUP)] = rows

        @pl.when(g == 0)
        def _():
            xret[k, 0] = rows[0]

    xarrive(CHUNKS - 1)

    def turn(i, _):
        g = 1 - i
        accumulate(CHUNKS - 1, g)
        lower(CHUNKS - 1, g)

        def one(p, _):
            activate(g * GROUP + p)
            return 0

        lax.fori_loop(0, GROUP, one, 0)
        down(0, g)
        for here in range(2):

            @pl.when(g == here)
            def _():
                for p in order:
                    if p // GROUP == here:
                        send_back(0, 4, p)

        return 0

    lax.fori_loop(0, 2, turn, 0)

    def mixed(k, q):
        rows = xret[k, :, q * TILE : (q + 2) * TILE].reshape(256, width)
        both = dot(mix[q], rows)
        return both[:toks] + both[toks:]

    def combine(k, h):
        returned(k, h)
        if h == 4:
            total = mixed(k, 7)
            for d in range(2):
                span = slice(d * half, (d + 1) * half)
                rs_s[k, 3, d, span] = total[span].astype(BF16)
                rsend(k, 4, d)
            return
        rarrive(k, h + 1)
        for d in range(2):
            total = mixed(k, place_of(h, d))
            if h == 3:
                span, rest = slice(d * half, (d + 1) * half), slice((1 - d) * half, (2 - d) * half)
                rs_s[k, 2, d, rest] = total[rest].astype(BF16)
                rs_s[k, 2, d, span] = (total[span] + rs_r[k, 3, d, span].astype(F32)).astype(BF16)
            else:
                rs_s[k, h - 1, d] = (total + rs_r[k, h, d].astype(F32)).astype(BF16)
            rsend(k, h, d)
        if h == 1:
            own[k] = mixed(k, 0)

    def finish(k):
        rarrive(k, 1)
        total = own[k] + rs_r[k, 0, 0].astype(F32) + rs_r[k, 0, 1].astype(F32)
        col = pl.multiple_of(chunk_column(k, z) * width, width)
        out_ref[:, pl.ds(col, width)] = total.astype(BF16)

    def slot_b(t, _):
        for h in range(1, 5):

            @pl.when(t == 2 * h - 2)
            def _():
                zarrive(WOUT, h)
                if h < 4:
                    zsend(WOUT, h + 1)

        @pl.when((t >= 1) & (t < CHUNKS))
        def _():
            def group(g, _):
                down(t, g)
                return 0

            lax.fori_loop(0, PEERS // GROUP, group, 0)
            for p in order:
                send_back(t, 4, p)

        for h in range(3, 0, -1):
            k = t - (4 - h)

            @pl.when((k >= 0) & (k < CHUNKS))
            def _():
                for p in order:
                    send_back(k, h, p)

        done = t - LAG - 4

        @pl.when(done >= 0)
        def _():
            finish(done)

        for h in range(1, 5):
            k = t - LAG - (4 - h)

            @pl.when((k >= 0) & (k < CHUNKS))
            def _():
                combine(k, h)

        return 0

    lax.fori_loop(0, CHUNKS + LAG + 4, slot_b, 0)

    await_bytes(xsend.at[:, pl.ds(1, PEERS - 1)], b_ss)
    await_bytes(tokbuf.at[:, pl.ds(0, 6)], y_ss.at[0])
    await_bytes(tokbuf.at[:, 7], y_ss.at[1])
    await_bytes(rs_s.at[:, pl.ds(0, 3)], r_ss.at[0])
    await_bytes(rs_s.at[:, 3, 0], r_ss.at[1])
    await_bytes(meta.at[pl.ds(0, 7)], m_ss)
    await_bytes(code_r.at[pl.ds(1, PEERS - 1)], c_ss)
    for kind in range(4):
        await_bytes(kinds[kind].at[pl.ds(0, 7)], w_ss.at[kind])


def shards(
    tokens,
    chosen_expert_index,
    router_weight_logits,
    token_tenant_index,
    adapted,
    gate_up_weight,
    down_weight,
    adapter_input_factors,
    adapter_output_factors,
):
    toks, model = tokens.shape
    width = model // CHUNKS
    hidden = down_weight.shape[1]
    rank = adapter_input_factors.shape[2]
    block = NY * SLOTS
    vmem = pl.BlockSpec(memory_space=pltpu.VMEM)
    dma = pltpu.SemaphoreType.DMA
    return pl.pallas_call(
        layer_kernel,
        out_shape=jax.ShapeDtypeStruct((toks, model), BF16),
        in_specs=[vmem] * 4 + [pl.BlockSpec(memory_space=pltpu.SMEM)] + [vmem] * 4,
        out_specs=vmem,
        scratch_shapes=[
            pltpu.VMEM((CHUNKS, NY, toks, width), BF16),
            pltpu.VMEM((NY, 24, toks), F32),
            pltpu.VMEM((NY + 1, PEERS * TILE, 2 * toks), BF16),
            pltpu.VMEM((NY, 2 * toks, 256), BF16),
            pltpu.VMEM((CHUNKS, PEERS, block, width), BF16),
            pltpu.VMEM((CHUNKS, PEERS, block, width), BF16),
            pltpu.VMEM((TILE, PEERS * TILE), BF16),
            pltpu.VMEM((PEERS, TILE, PEERS * TILE), BF16),
            pltpu.VMEM((8, width, 2 * hidden), BF16),
            pltpu.VMEM((8, hidden, width), BF16),
            pltpu.VMEM((8, CHUNKS, rank, width), BF16),
            pltpu.VMEM((8, rank, hidden), BF16),
            pltpu.VMEM((8 * rank, 2 * hidden), BF16),
            pltpu.VMEM((PEERS // GROUP, GROUP * block, 2 * hidden + 8 * rank), F32),
            pltpu.VMEM((PEERS // GROUP, GROUP * block, hidden), BF16),
            pltpu.VMEM((CHUNKS, PEERS, block, width), BF16),
            pltpu.VMEM((CHUNKS, toks, width), F32),
            pltpu.VMEM((CHUNKS, 4, 2, toks, width), BF16),
            pltpu.VMEM((CHUNKS, 4, 2, toks, width), BF16),
            dma((2,)),
            dma((CHUNKS, 4)),
            dma,
            dma((4,)),
            dma,
            dma((CHUNKS,)),
            dma,
            dma,
            dma((4,)),
            dma((4, 4)),
            dma,
            dma((CHUNKS, 4)),
            dma((2,)),
            dma((CHUNKS, 4)),
        ],
        compiler_params=pltpu.CompilerParams(
            collective_id=0, has_side_effects=True, vmem_limit_bytes=60 * 1024 * 1024
        ),
        cost_estimate=pl.CostEstimate(flops=8 * 10**9, bytes_accessed=3 * 10**6, transcendentals=0),
    )(
        tokens,
        chosen_expert_index.T,
        router_weight_logits.T,
        token_tenant_index[None, :],
        adapted.T,
        gate_up_weight[0],
        down_weight[0],
        adapter_input_factors[0, 0],
        adapter_output_factors[0, 0],
    )


def solution(mesh):
    placed = (
        P(("expert", "store"), None),
        P(("expert", "store"), None),
        P(("expert", "store"), None),
        P(("expert", "store")),
        P(None, "expert"),
        P("expert", "store", None),
        P("expert", None, "store"),
        P("store", "expert", None, None),
        P("store", "expert", None, None),
    )
    return jax.shard_map(
        shards, mesh=mesh, in_specs=placed, out_specs=P(("expert", "store"), None), check_vma=False
    )
```

time: 177 us -> 154 us (0.87)
  Pallas kernels: 173 us -> 152 us
    pallas_call x1, Pallas kernels: 173 us -> 152 us  [shards(): pl.pallas_call(layer_kernel, out_shape=jax.ShapeDtypeStruct((toks, model)...]
where the time goes in v2:
time: 154 us
  Pallas kernels  152 us (99%)
  local copies, waits for them, and re-layouts  1.88 us (1%)
    pallas_call x1, Pallas kernels, shards(): pl.pallas_call(layer_kernel, out_shape=jax.ShapeDtypeStruct((toks, model)...  152 us

profile of v2, /device:TPU:1, one launch (start us, length us, event | category | flops | bytes accessed | tf_op | source)
XLA Modules:
  0.0 153.9 jit_solution(10623534904993076997)
XLA Ops:
  0.0 152.0 %shard_map.91 = bf16[128,2048]{1,0:T(8,128)(2,1)} custom-call(bf16[128,2048]{1,0:T(8,128)(2,1)} %tok_ref.1, s32[8,128]{1,0:T(8,128)} %bitcast.12, f32[8,128]{1,0:T(8,128)} %bitcast.13, s32[1,128]{1,0:T(1,128)} %bitcast.14, s32[1,8]{1,0:T(1,128)} %bitcast.15, bf16[256,768]{1,0:T(8,128)(2,1)} %bitcast.8, bf16[384,256]{1,0:T(8,128)(2,1)} %bitcast.9, ...), custom_call_target="tpu_custom_call" | custom-call | flops 8000000000 | bytes 3000000 | tf_op jit(solution)/shard_map/pallas_call | solution.py:505
  152.1 1.9 %copy.11 = bf16[128,2048]{1,0:T(8,128)(2,1)} copy(bf16[128,2048]{1,0:T(8,128)(2,1)} %shard_map.91) | data formatting | bytes 1048576

commit v3 on v2

--- a/solution.py
+++ b/solution.py
@@ -6,6 +6,7 @@
 from jax.sharding import PartitionSpec as P
 
 MESH = pl.DeviceIdType.MESH
+FIN, FUP, WIN, WOUT = range(4)
 NX, NY, NC = 4, 8, 2
 PEERS = NX * NC
 SLOTS = 18
@@ -13,6 +14,19 @@
 CHUNKS = 8
 GROUP = 4
 LAG = 2
+HOP = 2
+STAGGER = 1
+LAST_A = CHUNKS + 4 * HOP
+LAST_B = CHUNKS - 1 + LAG + 4 * HOP
+OWN_BACK = CHUNKS + 3 * STAGGER
+PLAN_A = (
+    (6, ((WIN, 1), (FIN, 1), (FUP, 1)), ((WIN, 2), (FIN, 2), (FUP, 2))),
+    (9, ((WIN, 2),), ((WIN, 3),)),
+    (10, ((FIN, 2), (FUP, 2)), ((FIN, 3), (FUP, 3))),
+    (12, ((WIN, 3), (FIN, 3), (FUP, 3)), ((WIN, 4), (FIN, 4), (FUP, 4))),
+    (13, (), ((WOUT, 1),)),
+    (14, ((FIN, 4), (FUP, 4)), ()),
+)
 F32, BF16 = jnp.float32, jnp.bfloat16
 
 
@@ -28,7 +42,7 @@
 def layer_kernel(
     tok_ref, idx_ref, logit_ref, ten_ref, adp_ref, win_ref, wout_ref, fin_ref, fup_ref, out_ref,
     tokbuf, meta, sel, mix, xsend, xrecv, code_s, code_r, winb, woutb, finb, fupb, wide, pre, act,
-    xret, own, rs_s, rs_r,
+    xret, rs_s, rs_r,
     y_ss, y_rs, m_ss, m_rs, x_ss, x_rs, c_ss, c_rs, w_ss, w_rs, b_ss, b_rs, r_ss, r_rs,
 ):
     toks = tok_ref.shape[0]
@@ -105,7 +119,6 @@
     pl.semaphore_wait(barrier, len(partners))
 
     kinds = (finb, fupb, winb, woutb)
-    FIN, FUP, WIN, WOUT = range(4)
 
     def zsend(kind, h):
         for d in range(2):
@@ -171,7 +184,7 @@
         code_r[0] = codes.astype(BF16)
 
     order = [4, 5, 2, 3, 6, 7, 1]
-    tiles = {h: (0 if h == 1 else 2 * h - 1, 2 * h + 1) for h in range(1, 5)}
+    tiles = {h: (max(0, 2 * h - 1), 2 * h + 1) for h in range(0, 5)}
 
     def rows_of(h):
         return pl.ds(tiles[h][0] * TILE, (tiles[h][1] - tiles[h][0]) * TILE)
@@ -218,7 +231,7 @@
 
     def slot_a(t, _):
         for h in range(4, 0, -1):
-            k = t - h
+            k = t - HOP * h
 
             @pl.when((k >= 0) & (k < CHUNKS))
             def _():
@@ -242,74 +255,61 @@
 
         for h in range(0, 5):
 
-            @pl.when(t == h)
+            @pl.when(t == HOP * h)
             def _():
                 for q in range(max(0, 2 * h - 1), min(2 * h, 7) + 1):
                     build(q)
 
         for h in range(4, 0, -1):
-            k = t - h
+            k = t - HOP * h
 
             @pl.when((k >= 0) & (k < CHUNKS))
             def _():
                 select(k, h)
 
-        @pl.when(t == 4)
+        @pl.when(t < CHUNKS // 2)
+        def _():
+            for i in range(2):
+                select(2 * t + i, 0)
+
+        @pl.when(t == 4 * HOP)
         def _():
             tenants()
             for p in order:
                 remote(code_s, code_r.at[p], c_ss, c_rs, away(p)).start()
-            for kind in (WIN, FIN, FUP):
-                zarrive(kind, 1)
-                zsend(kind, 2)
-
-        @pl.when(t == 6)
-        def _():
-            zarrive(WIN, 2)
-            zsend(WIN, 3)
-
-        @pl.when(t == 7)
-        def _():
-            for kind in (FIN, FUP):
-                zarrive(kind, 2)
-                zsend(kind, 3)
-
-        @pl.when(t == 8)
-        def _():
-            zarrive(WIN, 3)
-            zsend(WIN, 4)
-
-        @pl.when(t == 9)
-        def _():
-            for kind in (FIN, FUP):
-                zarrive(kind, 3)
-                zsend(kind, 4)
-
-        @pl.when(t == 10)
-        def _():
-            zarrive(WIN, 4)
-            zsend(WOUT, 1)
-            for kind in (FIN, FUP):
-                zarrive(kind, 4)
+
+        for slot, came, goes in PLAN_A:
+
+            @pl.when(t == slot)
+            def _():
+                for kind, h in came:
+                    zarrive(kind, h)
+                for kind, h in goes:
+                    zsend(kind, h)
+
+        @pl.when(t == LAST_A - 2)
+        def _():
             lower_of(0, 4)
 
-        @pl.when(t == 11)
+        @pl.when(t == LAST_A - 1)
         def _():
             lower_of(4, 6)
 
-        @pl.when(t >= 5)
-        def _():
-            xarrive(t - 5)
+        done = t - 4 * HOP - 1
+
+        @pl.when(done >= 0)
+        def _():
+            xarrive(done)
 
             def group(g, _):
-                accumulate(t - 5, g)
+                accumulate(done, g)
                 return 0
 
             lax.fori_loop(0, PEERS // GROUP, group, 0)
 
         return 0
 
-    lax.fori_loop(0, CHUNKS + 4, slot_a, 0)
+    lax.fori_loop(0, LAST_A, slot_a, 0)
 
     for u in range(8):
         r = u * rank
@@ -317,7 +317,10 @@
         wide[r : r + rank // 2, hidden:] = jnp.zeros((rank // 2, hidden), BF16)
         wide[r + rank // 2 : r + rank, 0:hidden] = jnp.zeros((rank // 2, hidden), BF16)
         wide[r + rank // 2 : r + rank, hidden:] = fupb[u, rank // 2 :]
+    zarrive(WIN, 4)
     lower_of(6, 7)
+    zarrive(WOUT, 1)
+    zsend(WOUT, 2)
     await_bytes(code_r.at[pl.ds(1, PEERS - 1)], c_rs)
     lane_rank = lax.broadcasted_iota(jnp.int32, (1, 8 * rank), 1) // rank
     adapted = jnp.zeros((1, 8 * rank), F32)
@@ -348,11 +351,11 @@
 
     def send_back(k, h, p):
         remote(
-            xsend.at[k, p, rows_of(h)], xret.at[k, p, rows_of(h)], b_ss, b_rs.at[k, h - 1], back(p)
+            xsend.at[k, p, rows_of(h)], xret.at[k, p, rows_of(h)], b_ss, b_rs.at[k, h], back(p)
         ).start()
 
     def returned(k, h):
-        await_bytes(xret.at[k, pl.ds(1, PEERS - 1), rows_of(h)], b_rs.at[k, h - 1])
+        await_bytes(xret.at[k, pl.ds(1, PEERS - 1), rows_of(h)], b_rs.at[k, h])
 
     def rsend(k, h, d):
         src, dst = rs_s.at[k, h - 1, d], rs_r.at[k, h - 1, d]
@@ -420,17 +423,16 @@
             else:
                 rs_s[k, h - 1, d] = (total + rs_r[k, h, d].astype(F32)).astype(BF16)
             rsend(k, h, d)
-        if h == 1:
-            own[k] = mixed(k, 0)
 
     def finish(k):
         rarrive(k, 1)
-        total = own[k] + rs_r[k, 0, 0].astype(F32) + rs_r[k, 0, 1].astype(F32)
+        returned(k, 0)
+        total = mixed(k, 0) + rs_r[k, 0, 0].astype(F32) + rs_r[k, 0, 1].astype(F32)
         col = pl.multiple_of(chunk_column(k, z) * width, width)
         out_ref[:, pl.ds(col, width)] = total.astype(BF16)
 
     def slot_b(t, _):
-        for h in range(1, 5):
+        for h in range(2, 5):
 
             @pl.when(t == 2 * h - 2)
             def _():
@@ -449,29 +451,38 @@
                 send_back(t, 4, p)
 
         for h in range(3, 0, -1):
-            k = t - (4 - h)
+            k = t - STAGGER * (4 - h)
 
             @pl.when((k >= 0) & (k < CHUNKS))
             def _():
                 for p in order:
                     send_back(k, h, p)
 
-        done = t - LAG - 4
+        early = t - OWN_BACK
+
+        @pl.when((early >= 0) & (early < CHUNKS // 2))
+        def _():
+            for i in range(2):
+                for p in order:
+                    send_back(2 * early + i, 0, p)
+
+        for h in range(1, 5):
+            k = t - LAG - HOP * (4 - h)
+
+            @pl.when((k >= 0) & (k < CHUNKS))
+            def _():
+                combine(k, h)
+
+        done = t - (LAST_B - CHUNKS // 2)
 
         @pl.when(done >= 0)
         def _():
-            finish(done)
-
-        for h in range(1, 5):
-            k = t - LAG - (4 - h)
-
-            @pl.when((k >= 0) & (k < CHUNKS))
-            def _():
-                combine(k, h)
+            finish(2 * done)
+            finish(2 * done + 1)
 
         return 0
 
-    lax.fori_loop(0, CHUNKS + LAG + 4, slot_b, 0)
+    lax.fori_loop(0, LAST_B, slot_b, 0)
 
     await_bytes(xsend.at[:, pl.ds(1, PEERS - 1)], b_ss)
     await_bytes(tokbuf.at[:, pl.ds(0, 6)], y_ss.at[0])
@@ -524,7 +535,6 @@
             pltpu.VMEM((PEERS // GROUP, GROUP * block, 2 * hidden + 8 * rank), F32),
             pltpu.VMEM((PEERS // GROUP, GROUP * block, hidden), BF16),
             pltpu.VMEM((CHUNKS, PEERS, block, width), BF16),
-            pltpu.VMEM((CHUNKS, toks, width), F32),
             pltpu.VMEM((CHUNKS, 4, 2, toks, width), BF16),
             pltpu.VMEM((CHUNKS, 4, 2, toks, width), BF16),
             dma((2,)),
@@ -538,7 +548,7 @@
             dma((4,)),
             dma((4, 4)),
             dma,
-            dma((CHUNKS, 4)),
+            dma((CHUNKS, 5)),
             dma((2,)),
             dma((CHUNKS, 4)),
         ],

time: 154 us -> 141 us (0.916)
  Pallas kernels: 152 us -> 139 us
    pallas_call x1, Pallas kernels: 152 us -> 139 us  [shards(): pl.pallas_call(layer_kernel, out_shape=jax.ShapeDtypeStruct((toks, model)...]
where the time goes in v3:
time: 141 us
  Pallas kernels  139 us (99%)
  local copies, waits for them, and re-layouts  1.88 us (1%)
    pallas_call x1, Pallas kernels, shards(): pl.pallas_call(layer_kernel, out_shape=jax.ShapeDtypeStruct((toks, model)...  139 us

profile of v3, /device:TPU:1, one launch (start us, length us, event | category | flops | bytes accessed | tf_op | source)
XLA Modules:
  0.0 140.9 jit_solution(11655477506997232726)
XLA Ops:
  0.0 139.0 %shard_map.91 = bf16[128,2048]{1,0:T(8,128)(2,1)} custom-call(bf16[128,2048]{1,0:T(8,128)(2,1)} %tok_ref.1, s32[8,128]{1,0:T(8,128)} %bitcast.12, f32[8,128]{1,0:T(8,128)} %bitcast.13, s32[1,128]{1,0:T(1,128)} %bitcast.14, s32[1,8]{1,0:T(1,128)} %bitcast.15, bf16[256,768]{1,0:T(8,128)(2,1)} %bitcast.8, bf16[384,256]{1,0:T(8,128)(2,1)} %bitcast.9, ...), custom_call_target="tpu_custom_call" | custom-call | flops 8000000000 | bytes 3000000 | tf_op jit(solution)/shard_map/pallas_call | solution.py:516
  139.0 1.9 %copy.11 = bf16[128,2048]{1,0:T(8,128)(2,1)} copy(bf16[128,2048]{1,0:T(8,128)(2,1)} %shard_map.91) | data formatting | bytes 1048576

commit v4 on v3

--- a/solution.py
+++ b/solution.py
@@ -20,11 +20,11 @@
 LAST_B = CHUNKS - 1 + LAG + 4 * HOP
 OWN_BACK = CHUNKS + 3 * STAGGER
 PLAN_A = (
-    (6, ((WIN, 1), (FIN, 1), (FUP, 1)), ((WIN, 2), (FIN, 2), (FUP, 2))),
-    (9, ((WIN, 2),), ((WIN, 3),)),
-    (10, ((FIN, 2), (FUP, 2)), ((FIN, 3), (FUP, 3))),
-    (12, ((WIN, 3), (FIN, 3), (FUP, 3)), ((WIN, 4), (FIN, 4), (FUP, 4))),
-    (13, (), ((WOUT, 1),)),
+    (7, ((WIN, 1), (FIN, 1), (FUP, 1)), ((WIN, 2), (FIN, 2), (FUP, 2))),
+    (10, ((WIN, 2),), ((WIN, 3),)),
+    (11, ((FIN, 2), (FUP, 2)), ((FIN, 3), (FUP, 3))),
+    (12, ((WIN, 3),), ((WIN, 4),)),
+    (13, ((FIN, 3), (FUP, 3)), ((FIN, 4), (FUP, 4), (WOUT, 1))),
     (14, ((FIN, 4), (FUP, 4)), ()),
 )
 F32, BF16 = jnp.float32, jnp.bfloat16

time: 141 us -> 143 us (1.014)
  Pallas kernels: 139 us -> 141 us
    pallas_call x1, Pallas kernels: 139 us -> 141 us  [shards(): pl.pallas_call(layer_kernel, out_shape=jax.ShapeDtypeStruct((toks, model)...]
where the time goes in v4:
time: 143 us
  Pallas kernels  141 us (99%)
  local copies, waits for them, and re-layouts  1.88 us (1%)
    pallas_call x1, Pallas kernels, shards(): pl.pallas_call(layer_kernel, out_shape=jax.ShapeDtypeStruct((toks, model)...  141 us

profile of v4, /device:TPU:1, one launch (start us, length us, event | category | flops | bytes accessed | tf_op | source)
XLA Modules:
  0.0 142.6 jit_solution(16678072257811147687)
XLA Ops:
  0.0 140.7 %shard_map.91 = bf16[128,2048]{1,0:T(8,128)(2,1)} custom-call(bf16[128,2048]{1,0:T(8,128)(2,1)} %tok_ref.1, s32[8,128]{1,0:T(8,128)} %bitcast.12, f32[8,128]{1,0:T(8,128)} %bitcast.13, s32[1,128]{1,0:T(1,128)} %bitcast.14, s32[1,8]{1,0:T(1,128)} %bitcast.15, bf16[256,768]{1,0:T(8,128)(2,1)} %bitcast.8, bf16[384,256]{1,0:T(8,128)(2,1)} %bitcast.9, ...), custom_call_target="tpu_custom_call" | custom-call | flops 8000000000 | bytes 3000000 | tf_op jit(solution)/shard_map/pallas_call | solution.py:516
  140.7 1.9 %copy.11 = bf16[128,2048]{1,0:T(8,128)(2,1)} copy(bf16[128,2048]{1,0:T(8,128)(2,1)} %shard_map.91) | data formatting | bytes 1048576
